TPU v7x, 32 devices: a whole 2x2x4 slice. The times are simulated.
32 devices in a mesh: sub: 8 (over z, core), dom: 4 (over y, x).
Axes of the slice: x: 2, y: 2, z: 4, core: 2. Of those that a mesh axis runs over, the one named last changes fastest.
Arguments:
- start_vectors: float32 [8, 3, 64, 4, 16, 128], P('sub', None, None, 'dom'), may hold values from -6 to 6
- face_x: float32 [8, 4, 16, 128], P('sub', 'dom'), may hold values from 0.1 to 10
- face_y: float32 [8, 4, 16, 128], P('sub', 'dom'), may hold values from 0.1 to 10
- face_z: float32 [8, 4, 16, 128], P('sub', 'dom'), may hold values from 0.1 to 10
- masses: float32 [8, 4, 16, 128], P('sub', 'dom'), may hold values from 0.5 to 2
- active: int32 [8], P('sub'), may hold values from 8 to 16, as said below
Outputs:
- deflation: bfloat16 [8, 3, 64, 4, 16, 128], P('sub', None, None, 'dom')
- coarse_diag: float32 [8, 64, 64], P('sub')
- coarse_off: float32 [8, 64, 64], P('sub')
Inputs may be any that keep to these rules, and one draw needn't show every extreme that they name: `active`: some subdomain has all 16 planes.
All inputs are finite; a program needn't handle non-finite values.
Results may differ from a plain program's by a relative error of at most 0.001.
Values sent between devices are 32-bit elements; how exact they have to be, the bound alone decides.
A program may use at most 64 MiB of HBM per device.

v0:
```python
import jax
import jax.numpy as jnp
from jax import lax
from jax.sharding import PartitionSpec as P

OV = 4
STEPS = 2


def from_behind(value, axis, steps):
    count = lax.axis_size(axis)
    leading, last = (max(0, -steps), min(count, count - steps))
    return lax.ppermute(value, axis, [(source, source + steps) for source in range(leading, last)])


def with_halo(cells, sides, width):
    for axis, dim in sides:
        count = lax.axis_size(axis)
        ends = count - 1
        head = lax.slice_in_dim(cells, 0, width, axis=dim)
        tail = lax.slice_in_dim(cells, cells.shape[dim] - width, cells.shape[dim], axis=dim)
        cells = jnp.concatenate(
            [
                lax.ppermute(tail, axis, [(i, (i + 1) % count) for i in range(ends)]),
                cells,
                lax.ppermute(head, axis, [((i + 1) % count, i) for i in range(ends)]),
            ],
            axis=dim,
        )
    return cells


def gram_of(left, right):
    return jnp.einsum("ckyxz,clyxz->kl", left, right, precision=lax.Precision.HIGHEST)


def mix_cols(values, matrix):
    return jnp.einsum("ckyxz,kl->clyxz", values, matrix, precision=lax.Precision.HIGHEST)


def inverse_factor(gram_b):
    factor = jnp.linalg.cholesky(gram_b)
    identity = jnp.eye(gram_b.shape[0], dtype=jnp.float32)
    return lax.linalg.triangular_solve(factor, identity, left_side=True, lower=True)


def face_terms(values, weights, along):
    length = values.shape[along]
    head_part = lax.slice_in_dim(values, 0, length - 1, axis=along)
    tail_part = lax.slice_in_dim(values, 1, length, axis=along)
    fluxes = lax.slice_in_dim(weights, 0, length - 1, axis=along - 2)[None, None] * (
        head_part - tail_part
    )
    pad_after = [(0, 0)] * 5
    pad_after[along] = (0, 1)
    pad_before = [(0, 0)] * 5
    pad_before[along] = (1, 0)
    return jnp.pad(fluxes, pad_after) - jnp.pad(fluxes, pad_before)


def lower_faces(weights, along):
    length = weights.shape[along]
    widths = [(0, 0)] * 3
    widths[along] = (1, 0)
    return jnp.pad(lax.slice_in_dim(weights, 0, length - 1, axis=along), widths)


def matmul_high(left, right):
    return jnp.dot(left, right, precision=lax.Precision.HIGHEST)


def on_device(start_vectors, face_x, face_y, face_z, masses, active):
    start = start_vectors[0]
    own_x = face_x[0]
    own_y = face_y[0]
    own_z = face_z[0]
    own_mass = masses[0]
    active_now = active[0]
    rows_local = own_y.shape[0]
    planes_all = own_y.shape[1]
    depth_all = own_y.shape[2]
    rows_total = rows_local * lax.axis_size("dom")
    row_index = lax.axis_index("dom") * rows_local + jnp.arange(rows_local, dtype=jnp.int32)
    plane_index = jnp.arange(planes_all, dtype=jnp.int32)
    depth_index = jnp.arange(depth_all, dtype=jnp.int32)
    inside = (plane_index < active_now)[None, :, None]
    keep_x = (plane_index + 1 < active_now)[None, :, None]
    keep_y = inside & (row_index + 1 < rows_total)[:, None, None]
    keep_z = inside & (depth_index + 1 < depth_all)[None, None, :]
    live_x = own_x * keep_x.astype(jnp.float32)
    live_y = own_y * keep_y.astype(jnp.float32)
    live_z = own_z * keep_z.astype(jnp.float32)
    below_row = from_behind(live_y, "dom", 1)
    lower_y = jnp.concatenate([below_row, live_y[:-1]], axis=0)
    diagonal = (
        live_x
        + lower_faces(live_x, 1)
        + live_y
        + lower_y
        + live_z
        + lower_faces(live_z, 2)
        + own_mass
    )
    unity = jnp.clip(
        jnp.minimum(plane_index + 1, active_now - plane_index).astype(jnp.float32) / (OV + 1),
        0.0,
        1.0,
    )[None, :, None]
    b_weight = (own_mass * unity * unity)[None, None]

    def operate(values):
        padded = with_halo(values, (("dom", 2),), 1)
        result = live_y[None, None] * (values - padded[:, :, 2:]) + lower_y[None, None] * (
            values - padded[:, :, :-2]
        )
        return result + face_terms(values, live_x, 3) + face_terms(values, live_z, 4)

    vectors = start * inside.astype(jnp.float32)[None, None]
    for repeat in range(STEPS):
        image_raw = operate(vectors)
        gram_b, gram_a = lax.psum(
            (gram_of(vectors, b_weight * vectors), gram_of(vectors, image_raw)), "dom"
        )
        inv_now = inverse_factor(gram_b)
        ortho = mix_cols(vectors, inv_now.T)
        image = mix_cols(image_raw, inv_now.T)
        rayleigh = matmul_high(matmul_high(inv_now, gram_a), inv_now.T)
        residual = image - mix_cols(b_weight * ortho, rayleigh)
        vectors = ortho - 0.5 * residual / diagonal[None, None]
    weighted = unity[None, None] * vectors
    image_raw = operate(weighted)
    planes = lax.dynamic_slice_in_dim(image_raw, active_now - OV, OV, axis=3)
    neighbour = from_behind(planes, "sub", 1)
    gram_b, diag_raw, off_raw = lax.psum(
        (
            gram_of(vectors, b_weight * vectors),
            gram_of(weighted, image_raw),
            gram_of(weighted[:, :, :, :OV], neighbour),
        ),
        "dom",
    )
    inv_now = inverse_factor(gram_b)
    previous_inv = from_behind(inv_now, "sub", 1)
    deflate = mix_cols(weighted, inv_now.T)
    coarse_diag = matmul_high(matmul_high(inv_now, diag_raw), inv_now.T)
    coarse_off = matmul_high(matmul_high(inv_now, off_raw), previous_inv.T)
    return (deflate.astype(jnp.bfloat16)[None], coarse_diag[None], coarse_off[None])


def solution(mesh):
    placed = (
        P("sub", None, None, "dom", None, None),
        P("sub", "dom", None, None),
        P("sub", "dom", None, None),
        P("sub", "dom", None, None),
        P("sub", "dom", None, None),
        P("sub"),
    )
    return jax.shard_map(
        on_device,
        mesh=mesh,
        in_specs=placed,
        out_specs=(
            P("sub", None, None, "dom", None, None),
            P("sub", None, None),
            P("sub", None, None),
        ),
        check_vma=False,
    )
```

profile of v0, /device:TPU:8, one launch (start us, length us, event | category | flops | bytes accessed | tf_op | source)
XLA Modules:
  0.0 332.1 jit_solution(418359090972880745)
XLA Ops:
  1.3 2.0 bitcast_multiply_fusion.5
  3.4 4.6 %collective-permute-start.2 = (f32[3,64,1,16,128]{4,1,3,0,2:T(8,128)S(1)}, f32[3,64,1,16,128]{4,1,3,0,2:T(8,128)}, u32[]{:S(2)}, u32[]{:S(2)}) collective-permute-start(f32[3,64,1,16,128]{4,1,3,0,2:T(8,128)S(1)} %bitcast_multiply_fusion.5), channel_id=1, source_target_pairs={{0,1},{1,2},{2,3},{4,5},{5,6},{6,7},{8,9},{9,10},{10,11},{12,13},{... | collective-permute-start | bytes 4718600 | tf_op jit(solution)/shard_map/ppermute | solution.py:24
  7.9 1.3 collective-permute-start
  9.3 4.5 %collective-permute-start.1 = (f32[1,16,128]{2,1,0:T(8,128)S(1)}, f32[1,16,128]{2,1,0:T(8,128)S(1)}, u32[]{:S(2)}, u32[]{:S(2)}) collective-permute-start(f32[1,16,128]{2,1,0:T(8,128)S(1)} %bitcast_multiply_fusion.10), channel_id=1, source_target_pairs={{0,1},{1,2},{2,3},{4,5},{5,6},{6,7},{8,9},{9,10},{10,11},{12,13},{... | collective-permute-start | bytes 24584 | tf_op jit(solution)/shard_map/ppermute | solution.py:13
  14.8 2.2 fusion.51
  17.2 1.4 bitcast_multiply_fusion.8
  19.2 21.4 %collective-permute-done.1 = f32[1,16,128]{2,1,0:T(8,128)S(1)} collective-permute-done((f32[1,16,128]{2,1,0:T(8,128)S(1)}, f32[1,16,128]{2,1,0:T(8,128)S(1)}, u32[]{:S(2)}, u32[]{:S(2)}) %collective-permute-start.1) | collective-permute-done | bytes 8224 | tf_op jit(solution)/shard_map/ppermute | solution.py:13
  40.7 35.6 %collective-permute-done = f32[3,64,1,16,128]{4,1,3,0,2:T(8,128)} collective-permute-done((f32[3,64,1,16,128]{4,1,3,0,2:T(8,128)S(1)}, f32[3,64,1,16,128]{4,1,3,0,2:T(8,128)}, u32[]{:S(2)}, u32[]{:S(2)}) %collective-permute-start) | collective-permute-done | bytes 1572896 | tf_op jit(solution)/shard_map/ppermute | solution.py:26
  76.2 3.2 subtract_add_fusion.2
  79.4 1.1 copy-done.3
  80.6 1.7 fusion.56
  82.3 16.3 %all-reduce.16 = (f32[64,64]{0,1:T(8,128)S(1)}, f32[64,64]{1,0:T(8,128)S(1)}) all-reduce(f32[64,64]{0,1:T(8,128)S(1)} %fusion.51, f32[64,64]{1,0:T(8,128)S(1)} %fusion.56), channel_id=1, replica_groups=mesh['sub'=8,'dom'=4] {'dom'}, use_global_device_ids=true, to_apply=%region_0.1 | all-reduce | flops 8192 | bytes 65536 | tf_op jit(solution)/shard_map/psum | solution.py:121
  98.7 5.8 %cholesky.59 = f32[64,64]{1,0:T(8,128)S(1)} custom-call(f32[64,64]{1,0:T(8,128)S(1)} %fusion.106), custom_call_target="Cholesky" | custom-call | tf_op jit(solution)/shard_map/jit(cholesky)/cholesky | solution.py:42
  105.9 4.9 %custom-call.7 = f32[1,64,64]{1,2,0:T(8,128)S(1)} custom-call(f32[1,64,64]{2,1,0:T(8,128)S(1)} %fusion.93), custom_call_target="InvertDiagBlocksLowerTriangular" | custom-call | tf_op jit(solution)/shard_map/triangular_solve/custom-call.0 | solution.py:44
  111.0 1.9 fusion.31
  113.3 1.4 fusion.7
  114.7 1.7 fusion.26
  116.4 1.3 collective-permute-start.3
  117.7 4.6 %collective-permute-start.4 = (f32[3,64,1,16,128]{4,1,3,0,2:T(8,128)S(1)}, f32[3,64,1,16,128]{4,1,3,0,2:T(8,128)S(1)}, u32[]{:S(2)}, u32[]{:S(2)}) collective-permute-start(f32[3,64,1,16,128]{4,1,3,0,2:T(8,128)S(1)} %bitcast.267), channel_id=1, source_target_pairs={{0,1},{1,2},{2,3},{4,5},{5,6},{6,7},{8,9},{9,10},{10,11},{12,13},{... | collective-permute-start | bytes 4718600 | tf_op jit(solution)/shard_map/ppermute | solution.py:24
  122.4 1.4 fusion.61
  124.5 31.1 %collective-permute-done.3 = f32[3,64,1,16,128]{4,1,3,0,2:T(8,128)S(1)} collective-permute-done((f32[3,64,1,16,128]{4,1,3,0,2:T(8,128)S(1)}, f32[3,64,1,16,128]{4,1,3,0,2:T(8,128)S(1)}, u32[]{:S(2)}, u32[]{:S(2)}) %collective-permute-start.3) | collective-permute-done | bytes 1572896 | tf_op jit(solution)/shard_map/ppermute | solution.py:26
  155.7 1.1 subtract_add_fusion.1
  156.8 1.1 copy-done.1
  157.9 1.4 fusion.66
  159.3 43.8 %all-reduce.15 = (f32[64,64]{0,1:T(8,128)S(1)}, f32[64,64]{1,0:T(8,128)S(1)}) all-reduce(f32[64,64]{0,1:T(8,128)S(1)} %fusion.61, f32[64,64]{1,0:T(8,128)S(1)} %fusion.66), channel_id=1, replica_groups=mesh['sub'=8,'dom'=4] {'dom'}, use_global_device_ids=true, to_apply=%region_4.7 | all-reduce | flops 8192 | bytes 65536 | tf_op jit(solution)/shard_map/psum | solution.py:121
  203.2 5.8 %cholesky.70 = f32[64,64]{1,0:T(8,128)S(1)} custom-call(f32[64,64]{1,0:T(8,128)S(1)} %fusion.102), custom_call_target="Cholesky" | custom-call | tf_op jit(solution)/shard_map/jit(cholesky)/cholesky | solution.py:42
  210.4 4.9 %custom-call.8 = f32[1,64,64]{1,2,0:T(8,128)S(1)} custom-call(f32[1,64,64]{2,1,0:T(8,128)S(1)} %fusion.94), custom_call_target="InvertDiagBlocksLowerTriangular" | custom-call | tf_op jit(solution)/shard_map/triangular_solve/custom-call.0 | solution.py:44
  215.5 1.5 fusion.18
  217.4 1.4 fusion.5
  218.8 1.8 bitcast_multiply_fusion.1
  220.7 3.5 %collective-permute-start.6 = (f32[3,64,1,16,128]{4,1,3,0,2:T(8,128)S(1)}, f32[3,64,1,16,128]{4,1,3,0,2:T(8,128)}, u32[]{:S(2)}, u32[]{:S(2)}) collective-permute-start(f32[3,64,1,16,128]{4,1,3,0,2:T(8,128)S(1)} %get-tuple-element.21), channel_id=1, source_target_pairs={{0,1},{1,2},{2,3},{4,5},{5,6},{6,7},{8,9},{9,10},{10,11},{12,13},{... | collective-permute-start | bytes 4718600 | tf_op jit(solution)/shard_map/ppermute | solution.py:24
  224.2 1.3 collective-permute-start.5
  226.2 21.2 %collective-permute-done.6 = f32[3,64,1,16,128]{4,1,3,0,2:T(8,128)} collective-permute-done((f32[3,64,1,16,128]{4,1,3,0,2:T(8,128)S(1)}, f32[3,64,1,16,128]{4,1,3,0,2:T(8,128)}, u32[]{:S(2)}, u32[]{:S(2)}) %collective-permute-start.6) | collective-permute-done | bytes 1572896 | tf_op jit(solution)/shard_map/ppermute | solution.py:24
  247.4 36.3 %collective-permute-done.5 = f32[3,64,1,16,128]{4,1,3,0,2:T(8,128)} collective-permute-done((f32[3,64,1,16,128]{4,1,3,0,2:T(8,128)S(1)}, f32[3,64,1,16,128]{4,1,3,0,2:T(8,128)}, u32[]{:S(2)}, u32[]{:S(2)}) %collective-permute-start.5) | collective-permute-done | bytes 1572896 | tf_op jit(solution)/shard_map/ppermute | solution.py:26
  283.7 3.0 subtract_add_fusion
  286.7 1.9 collective-permute-start.7
  288.6 1.4 fusion.76
  290.1 1.4 fusion.71
  291.5 4.3 %collective-permute-done.7 = f32[3,64,1,4,128]{4,1,3,0,2:T(8,128)S(1)} collective-permute-done((f32[3,64,1,4,128]{4,1,3,0,2:T(8,128)S(1)}, f32[3,64,1,4,128]{4,1,3,0,2:T(8,128)S(1)}, u32[]{:S(2)}, u32[]{:S(2)}) %collective-permute-start.7) | collective-permute-done | bytes 393248 | tf_op jit(solution)/shard_map/ppermute | solution.py:13
  296.3 15.8 %all-reduce.14 = (f32[64,64]{0,1:T(8,128)S(1)}, f32[64,64]{1,0:T(8,128)S(1)}, f32[64,64]{1,0:T(8,128)S(1)}) all-reduce(f32[64,64]{0,1:T(8,128)S(1)} %fusion.76, f32[64,64]{1,0:T(8,128)S(1)} %fusion.71, f32[64,64]{1,0:T(8,128)S(1)} %convolution_bitcast_fusion.1), channel_id=1, replica_groups=mesh['sub'=8,'dom'=4] {'dom'}, use_global_device_ids=true, to_apply=%region_6.9 | all-reduce | flops 12288 | bytes 98304 | tf_op jit(solution)/shard_map/psum | solution.py:134
  312.2 5.8 %cholesky.81 = f32[64,64]{1,0:T(8,128)S(1)} custom-call(f32[64,64]{1,0:T(8,128)S(1)} %fusion.98), custom_call_target="Cholesky" | custom-call | tf_op jit(solution)/shard_map/jit(cholesky)/cholesky | solution.py:42
  319.4 4.9 %custom-call.9 = f32[1,64,64]{1,2,0:T(8,128)S(1)} custom-call(f32[1,64,64]{2,1,0:T(8,128)S(1)} %fusion.95), custom_call_target="InvertDiagBlocksLowerTriangular" | custom-call | tf_op jit(solution)/shard_map/triangular_solve/custom-call.0 | solution.py:44
  324.5 1.5 fusion.48
  326.0 1.9 collective-permute-start.8
  328.3 0.8 convolution_bitcast_fusion.2
  329.1 1.4 copy.19
  330.5 0.8 collective-permute-done.8
  331.3 0.8 convolution_bitcast_fusion
  (66 shorter events, 9.7 us)
Async XLA Ops:
  1.3 7.9 %copy-start.6 = (f32[1,1,16,128]{3,2,1,0:T(8,128)S(1)}, f32[1,1,16,128]{3,2,1,0:T(8,128)}, u32[]{:S(2)}) copy-start(f32[1,1,16,128]{3,2,1,0:T(8,128)} %param.11) | copy-start | bytes 24580
  1.3 12.6 %copy-start.8 = (f32[1,1,16,128]{3,2,1,0:T(8,128)S(1)}, f32[1,1,16,128]{3,2,1,0:T(8,128)}, u32[]{:S(2)}) copy-start(f32[1,1,16,128]{3,2,1,0:T(8,128)} %param.12) | copy-start | bytes 24580
  1.3 12.7 %copy-start.7 = (f32[1,1,16,128]{3,2,1,0:T(8,128)S(1)}, f32[1,1,16,128]{3,2,1,0:T(8,128)}, u32[]{:S(2)}) copy-start(f32[1,1,16,128]{3,2,1,0:T(8,128)} %param.13) | copy-start | bytes 24580
  1.3 12.7 %copy-start = (f32[1,3,64,1,16,128]{5,4,3,2,1,0:T(8,128)S(1)}, f32[1,3,64,1,16,128]{5,4,3,2,1,0:T(8,128)}, u32[]{:S(2)}) copy-start(f32[1,3,64,1,16,128]{5,4,3,2,1,0:T(8,128)} %param.9) | copy-start | bytes 4718596
  3.4 37.3 %collective-permute-start.2 = (f32[3,64,1,16,128]{4,1,3,0,2:T(8,128)S(1)}, f32[3,64,1,16,128]{4,1,3,0,2:T(8,128)}, u32[]{:S(2)}, u32[]{:S(2)}) collective-permute-start(f32[3,64,1,16,128]{4,1,3,0,2:T(8,128)S(1)} %bitcast_multiply_fusion.5), channel_id=1, source_target_pairs={{0,1},{1,2},{2,3},{4,5},{5,6},{6,7},{8,9},{9,10},{10,11},{12,13},{... | collective-permute-start | bytes 4718600 | tf_op jit(solution)/shard_map/ppermute | solution.py:24
  7.9 68.3 %collective-permute-start = (f32[3,64,1,16,128]{4,1,3,0,2:T(8,128)S(1)}, f32[3,64,1,16,128]{4,1,3,0,2:T(8,128)}, u32[]{:S(2)}, u32[]{:S(2)}) collective-permute-start(f32[3,64,1,16,128]{4,1,3,0,2:T(8,128)S(1)} %bitcast_multiply_fusion.5), channel_id=1, source_target_pairs={{1,0},{2,1},{3,2},{5,4},{6,5},{7,6},{9,8},{10,9},{11,10},{13,12},{... | collective-permute-start | bytes 4718600 | tf_op jit(solution)/shard_map/ppermute | solution.py:26
  9.3 31.3 %collective-permute-start.1 = (f32[1,16,128]{2,1,0:T(8,128)S(1)}, f32[1,16,128]{2,1,0:T(8,128)S(1)}, u32[]{:S(2)}, u32[]{:S(2)}) collective-permute-start(f32[1,16,128]{2,1,0:T(8,128)S(1)} %bitcast_multiply_fusion.10), channel_id=1, source_target_pairs={{0,1},{1,2},{2,3},{4,5},{5,6},{6,7},{8,9},{9,10},{10,11},{12,13},{... | collective-permute-start | bytes 24584 | tf_op jit(solution)/shard_map/ppermute | solution.py:13
  14.1 0.7 copy-start.9
  79.4 1.2 copy-start.3
  80.6 30.5 %copy-start.5 = (f32[3,64,16,128]{3,2,1,0:T(8,128)S(1)}, f32[3,64,16,128]{3,2,1,0:T(8,128)}, u32[]{:S(2)}) copy-start(f32[3,64,16,128]{3,2,1,0:T(8,128)} %bitcast_multiply_fusion.8) | copy-start | bytes 4718596
  113.3 1.4 copy-start.4
  116.4 39.2 %collective-permute-start.3 = (f32[3,64,1,16,128]{4,1,3,0,2:T(8,128)S(1)}, f32[3,64,1,16,128]{4,1,3,0,2:T(8,128)S(1)}, u32[]{:S(2)}, u32[]{:S(2)}) collective-permute-start(f32[3,64,1,16,128]{4,1,3,0,2:T(8,128)S(1)} %bitcast.266), channel_id=1, source_target_pairs={{1,0},{2,1},{3,2},{5,4},{6,5},{7,6},{9,8},{10,9},{11,10},{13,12},{... | collective-permute-start | bytes 4718600 | tf_op jit(solution)/shard_map/ppermute | solution.py:26
  117.7 37.9 %collective-permute-start.4 = (f32[3,64,1,16,128]{4,1,3,0,2:T(8,128)S(1)}, f32[3,64,1,16,128]{4,1,3,0,2:T(8,128)S(1)}, u32[]{:S(2)}, u32[]{:S(2)}) collective-permute-start(f32[3,64,1,16,128]{4,1,3,0,2:T(8,128)S(1)} %bitcast.267), channel_id=1, source_target_pairs={{0,1},{1,2},{2,3},{4,5},{5,6},{6,7},{8,9},{9,10},{10,11},{12,13},{... | collective-permute-start | bytes 4718600 | tf_op jit(solution)/shard_map/ppermute | solution.py:24
  156.8 1.2 copy-start.1
  217.4 1.4 copy-start.2
  220.7 26.7 %collective-permute-start.6 = (f32[3,64,1,16,128]{4,1,3,0,2:T(8,128)S(1)}, f32[3,64,1,16,128]{4,1,3,0,2:T(8,128)}, u32[]{:S(2)}, u32[]{:S(2)}) collective-permute-start(f32[3,64,1,16,128]{4,1,3,0,2:T(8,128)S(1)} %get-tuple-element.21), channel_id=1, source_target_pairs={{0,1},{1,2},{2,3},{4,5},{5,6},{6,7},{8,9},{9,10},{10,11},{12,13},{... | collective-permute-start | bytes 4718600 | tf_op jit(solution)/shard_map/ppermute | solution.py:24
  224.2 59.5 %collective-permute-start.5 = (f32[3,64,1,16,128]{4,1,3,0,2:T(8,128)S(1)}, f32[3,64,1,16,128]{4,1,3,0,2:T(8,128)}, u32[]{:S(2)}, u32[]{:S(2)}) collective-permute-start(f32[3,64,1,16,128]{4,1,3,0,2:T(8,128)S(1)} %get-tuple-element.21), channel_id=1, source_target_pairs={{1,0},{2,1},{3,2},{5,4},{6,5},{7,6},{9,8},{10,9},{11,10},{13,12},{... | collective-permute-start | bytes 4718600 | tf_op jit(solution)/shard_map/ppermute | solution.py:26
  286.7 9.1 %collective-permute-start.7 = (f32[3,64,1,4,128]{4,1,3,0,2:T(8,128)S(1)}, f32[3,64,1,4,128]{4,1,3,0,2:T(8,128)S(1)}, u32[]{:S(2)}, u32[]{:S(2)}) collective-permute-start(f32[3,64,1,4,128]{4,1,3,0,2:T(8,128)S(1)} %constant_dynamic-slice_fusion), channel_id=1, source_target_pairs={{0,4},{4,8},{8,12},{12,16},{16,20},{20,24},{24,28},{1,5},{5,9},{9,... | collective-permute-start | bytes 1179656 | tf_op jit(solution)/shard_map/ppermute | solution.py:13
  326.0 5.2 %collective-permute-start.8 = (f32[64,64]{1,0:T(8,128)S(1)}, f32[64,64]{1,0:T(8,128)S(1)}, u32[]{:S(2)}, u32[]{:S(2)}) collective-permute-start(f32[64,64]{1,0:T(8,128)S(1)} %fusion.87), channel_id=1, source_target_pairs={{0,4},{4,8},{8,12},{12,16},{16,20},{20,24},{24,28},{1,5},{5,9},{9,... | collective-permute-start | bytes 49160 | tf_op jit(solution)/shard_map/ppermute | solution.py:13
where the time goes:
time: 334 us; the launch traced here: 332 us
  waiting for transfers between devices  151 us (45%)
  blocking collectives  75.8 us (23%)
  other arithmetic  49.6 us (15%)
  starting transfers between devices  25 us (7%)
  matrix products  24.7 us (7%)
  local copies, waits for them, and re-layouts  4.41 us (1%)
    ppermute x3, waiting for transfers between devices, with_halo(): lax.ppermute(head, axis, [((i + 1) % count, i) for i in range(ends)])  103 us
    psum x2, blocking collectives, on_device(): lax.psum((gram_of(vectors, b_weight * vectors), gram_of(vectors, image_ra...  60 us
    ppermute x3, waiting for transfers between devices, from_behind(): lax.ppermute(value, axis, [(source, source + steps) for source in range(l...  26.5 us
    ppermute x3, waiting for transfers between devices, with_halo(): lax.ppermute(tail, axis, [(i, (i + 1) % count) for i in range(ends)])  21.2 us
    another operation x9, other arithmetic, inverse_factor(): factor = jnp.linalg.cholesky(gram_b)  19.6 us
    another operation x6, other arithmetic, inverse_factor(): lax.linalg.triangular_solve(factor, identity, left_side=True, lower=True)  16.6 us
    psum x1, blocking collectives, on_device(): lax.psum((gram_of(vectors, b_weight * vectors), gram_of(weighted, image_r...  15.8 us
    ppermute x3, starting transfers between devices, with_halo(): lax.ppermute(tail, axis, [(i, (i + 1) % count) for i in range(ends)])  12.7 us
  transfers between devices with their start and end apart: 9, of which 7 were waited for; matrix products, arithmetic and copies ran while one was open for 4% of the time, Pallas kernels for 0%

commit v1 on v0

v1 whole, which is shorter than its diff:
```python
import functools

import jax
import jax.numpy as jnp
from jax import lax
from jax.experimental import pallas as pl
from jax.experimental.pallas import tpu as pltpu
from jax.sharding import PartitionSpec as P

OV = 4
STEPS = 2
MESH = pl.DeviceIdType.MESH
F32 = jnp.float32
BF16 = jnp.bfloat16


def split(v):
    hi = v.astype(BF16)
    return hi, (v - hi.astype(F32)).astype(BF16)


def nt(a, b):
    return lax.dot_general(a, b, (((1,), (1,)), ((), ())), preferred_element_type=F32)


def exact(a, b, dims):
    return lax.dot_general(
        a, b, (dims, ((), ())), precision=lax.Precision.HIGHEST, preferred_element_type=F32
    )


def kernel(
    n, subs, comps, nk, nx,
    start, fx, fy, fz, mass, active,
    out, diag_out, off_out,
    sbuf, vec, img, home, rows32, cs, cr, dv, hs, hr, gr, gf, us, ur, fs, fr,
    s_sem, r_sem, cs_sem, cr_sem, hs_sem, hr_sem, gs_sem, gr_sem,
    ws_sem, wr_sem, us_sem, ur_sem,
):
    nz = fx.shape[1]
    group = nz // n
    nq = nx // n
    per = n * comps
    me = lax.axis_index("dom")
    sub = lax.axis_index("sub")
    peers = [lax.rem(me + d, n) for d in range(n)]
    right, left = peers[1], peers[n - 1]
    next_sub, prev_sub = lax.rem(sub + 1, subs), lax.rem(sub + subs - 1, subs)

    barrier = pltpu.get_barrier_semaphore()
    for d in range(1, n):
        pl.semaphore_signal(barrier, inc=1, device_id=(sub, peers[d]), device_id_type=MESH)
    for s in (next_sub, prev_sub):
        pl.semaphore_signal(barrier, inc=1, device_id=(s, me), device_id_type=MESH)

    a = active[0]
    lane = lax.broadcasted_iota(jnp.int32, (1, nz), 1)
    grp = lane // group
    zin = lane - grp * group

    pi = lax.broadcasted_iota(jnp.int32, (nx, nz), 0)
    zi = lax.broadcasted_iota(jnp.int32, (nx, nz), 1)
    kx = jnp.where(pi + 1 < a, fx[...], 0.0)
    ky = jnp.where((pi < a) & (me + 1 < n), fy[...], 0.0)
    kz = jnp.where((pi < a) & (zi + 1 < nz), fz[...], 0.0)
    lx = jnp.where(pi == 0, 0.0, pltpu.roll(kx, 1, 0))
    lz = jnp.where(zi == 0, 0.0, pltpu.roll(kz, 1, 1))
    coefs = (kx, lx, ky, kz, lz, mass[...])

    def regroup(blocks, e):
        res = blocks[0]
        for r in range(1, n):
            res = jnp.where(grp == lax.rem(e + r, n), blocks[r], res)
        return pltpu.roll(res, lax.rem(n - e, n) * group, 1)

    for ai, arr in enumerate(coefs):
        for q in range(nq):
            blocks = [
                pltpu.roll(jnp.broadcast_to(arr[q * n + r : q * n + r + 1], (8, nz)), r * group, 1)
                for r in range(n)
            ]
            for d in range(n):
                res = regroup(blocks, peers[d])
                if d == 0:
                    cr[me, ai, q] = res
                else:
                    cs[d, ai, q] = res

    pl.semaphore_wait(barrier, n - 1 + 2)

    def to_peer(src, dst, ss, rs, d):
        return pltpu.make_async_remote_copy(
            src_ref=src, dst_ref=dst, send_sem=ss, recv_sem=rs,
            device_id=(sub, peers[d]), device_id_type=MESH,
        )

    def to_next(src, dst, ss, rs):
        return pltpu.make_async_remote_copy(
            src_ref=src, dst_ref=dst, send_sem=ss, recv_sem=rs,
            device_id=(next_sub, me), device_id_type=MESH,
        )

    coef_copies = [
        to_peer(cs.at[d], cr.at[me], cs_sem.at[d], cr_sem.at[d], d) for d in range(1, n)
    ]
    for cp in coef_copies:
        cp.start()

    vec_copies = []
    for c in range(comps):
        def pack(q, _, c=c):
            blocks = []
            for r in range(n):
                x = q * n + r
                v = start[c, pl.ds(x, nk, stride=nx), :]
                blocks.append(pltpu.roll(jnp.where(x < a, v, 0.0), r * group, 1))
            for d in range(n):
                res = regroup(blocks, peers[d])
                if d == 0:
                    vec[me, c, q] = res
                else:
                    sbuf[d, c, q] = res
            return 0
        lax.fori_loop(0, nq, pack, 0)
        for d in range(1, n):
            cp = to_peer(sbuf.at[d, c], vec.at[me, c], s_sem.at[c, d], r_sem.at[c, d], d)
            cp.start()
            vec_copies.append(cp)

    for cp in coef_copies:
        cp.wait()

    for y in range(n):
        for q in range(nq):
            plane = q * n + grp
            ckx, clx, cky, ckz, clz, cm = (cr[y, ai, q] for ai in range(6))
            ly = cr[y - 1, 2, q] if y else jnp.zeros_like(cky)
            total = ckx + clx + cky + ly + ckz + clz
            unity = jnp.clip(
                jnp.minimum(plane + 1, a - plane).astype(F32) / (OV + 1), 0.0, 1.0
            )
            unity = jnp.broadcast_to(unity, total.shape)
            half = 0.5 / (total + cm)
            b = cm * unity * unity
            tail = ((plane >= a - OV) & (plane < a)).astype(F32)
            for i, arr in enumerate((total, ly, half, half * b, b, unity, jnp.broadcast_to(tail, total.shape))):
                dv[i, y, q] = arr

    for cp in vec_copies:
        cp.wait()

    def halo_copies(p):
        return (
            to_peer(hs.at[p, 0], hr.at[p, 0], hs_sem.at[p, 0], hr_sem.at[p, 0], n - 1),
            to_peer(hs.at[p, 1], hr.at[p, 1], hs_sem.at[p, 1], hr_sem.at[p, 1], 1),
        )

    def put_halo(p, y, c, q, v):
        b = (y * comps + c) * nq + q
        slot = lax.div(b, group)
        pos = b - slot * group
        lo = pltpu.roll(v, pos, 1)
        hi = pltpu.roll(v, lax.rem(pos + nz + 1 - group, nz), 1)
        here = zin == pos
        hs[p, 0, slot] = jnp.where(here, lo, hs[p, 0, slot])
        hs[p, 1, slot] = jnp.where(here, hi, hs[p, 1, slot])

    def row(ref, i, y, q):
        return ref[i, y, q][0:1]

    def apply_and_gram(p):
        def body(i, acc):
            y = lax.div(i, comps)
            c = i - y * comps
            yu, yd = jnp.minimum(y + 1, n - 1), jnp.maximum(y - 1, 0)
            vs = [vec[y, c, q] for q in range(nq)]
            ups = [pltpu.roll(v, nz - group, 1) for v in vs]
            downs = [pltpu.roll(v, group, 1) for v in vs]
            lefts, bvs = [], []
            for q in range(nq):
                v = vs[q]
                b = i * nq + q
                slot = lax.div(b, group)
                pos = b - slot * group
                xp = ups[q] if q + 1 == nq else jnp.where(grp == n - 1, ups[q + 1], ups[q])
                xm = downs[q] if q == 0 else jnp.where(grp == 0, downs[q - 1], downs[q])
                zp = jnp.where(
                    zin == group - 1, pltpu.roll(hr[p, 0, slot], group - 1 - pos, 1),
                    pltpu.roll(v, nz - 1, 1),
                )
                zm = jnp.where(
                    zin == 0, pltpu.roll(hr[p, 1, slot], lax.rem(nz - pos, nz), 1),
                    pltpu.roll(v, 1, 1),
                )
                def cf(ai):
                    return cr[y, ai, q][0:1]
                res = (
                    row(dv, 0, y, q) * v
                    - cf(0) * xp - cf(1) * xm
                    - cf(2) * vec[yu, c, q] - row(dv, 1, y, q) * vec[yd, c, q]
                    - cf(3) * zp - cf(4) * zm
                )
                img[y, c, q] = res
                lefts.append(res)
                bvs.append(v * (cf(5) if p == STEPS else row(dv, 4, y, q)))
            v_hi, v_lo = split(jnp.concatenate(vs, 1))
            b_hi, b_lo = split(jnp.concatenate(bvs, 1))
            a_hi, a_lo = split(jnp.concatenate(lefts, 1))
            return acc + nt(
                jnp.concatenate([v_hi, v_lo], 0),
                jnp.concatenate([b_hi, a_hi, b_lo, a_lo], 0),
            )

        acc = lax.fori_loop(0, per, body, jnp.zeros((2 * nk, 4 * nk), F32))
        return acc[:nk, : 2 * nk] + acc[:nk, 2 * nk :] + acc[nk:, : 2 * nk]

    def gather(ref, sems, make):
        copies = [
            to_peer(ref.at[me], ref.at[me], sems[0].at[d], sems[1].at[d], d) for d in range(1, n)
        ]
        for cp in copies:
            cp.start()
        for cp in copies:
            cp.wait()
        total = ref[0]
        for y in range(1, n):
            total = total + ref[y]
        return total

    hs[...] = jnp.zeros_like(hs)
    ri = lax.broadcasted_iota(jnp.int32, (nk, 1), 0)

    def pack_halo(i, _):
        y = lax.div(i, comps)
        c = i - y * comps
        for q in range(nq):
            put_halo(0, y, c, q, vec[y, c, q])
        return 0

    lax.fori_loop(0, per, pack_halo, 0)

    for p in range(STEPS):
        copies = halo_copies(p)
        for cp in copies:
            cp.start()
        for cp in copies:
            cp.wait()
        gr[p, me] = apply_and_gram(p)
        m = gather(gr.at[p], (gs_sem.at[p], gr_sem.at[p]), None)
        for j in range(nk):
            piv = m[j : j + 1, j : j + 1]
            line = m[j : j + 1, :] / piv
            m = jnp.where(ri == j, line, m - m[:, j : j + 1] * line)
        xt = m.T[nk:, :]
        x_hi, x_lo = split(xt)
        x3 = jnp.concatenate([x_hi, x_lo, x_hi], 1)

        def update(i, _, p=p, x3=x3):
            y = lax.div(i, comps)
            c = i - y * comps
            v = jnp.concatenate([vec[y, c, q] for q in range(nq)], 1)
            v_hi, v_lo = split(v)
            mixed = jnp.dot(
                x3, jnp.concatenate([v_hi, v_hi, v_lo], 0), preferred_element_type=F32
            )
            for q in range(nq):
                new = (
                    vec[y, c, q]
                    - row(dv, 2, y, q) * img[y, c, q]
                    + row(dv, 3, y, q) * mixed[:, q * nz : (q + 1) * nz]
                )
                if p == STEPS - 1:
                    new = new * row(dv, 5, y, q)
                vec[y, c, q] = new
                put_halo(p + 1, y, c, q, new)
            return 0

        lax.fori_loop(0, per, update, 0)

    copies = halo_copies(STEPS)
    for cp in copies:
        cp.start()
    back = []
    for d in range(1, n):
        cp = to_peer(vec.at[peers[d]], home.at[me], ws_sem.at[d], wr_sem.at[d], d)
        cp.start()
        back.append(cp)
    for cp in copies:
        cp.wait()
    both = apply_and_gram(STEPS)

    r0 = lax.rem(a - OV, n)

    def planes(i, _):
        y = lax.div(i, comps)
        c = i - y * comps
        u = img[y, c, 0] * row(dv, 6, y, 0)
        for q in range(1, nq):
            u = u + img[y, c, q] * row(dv, 6, y, q)
        bit = 1
        while bit < n:
            moved = pltpu.roll(u, nz - bit * group, 1)
            u = jnp.where(lax.rem(lax.div(r0, bit), 2) == 1, moved, u)
            bit *= 2
        us[y, c] = u
        return 0

    lax.fori_loop(0, per, planes, 0)
    ucopy = to_next(us, ur, us_sem.at[0], ur_sem.at[0])
    ucopy.start()
    ucopy.wait()

    def off_body(i, acc):
        y = lax.div(i, comps)
        c = i - y * comps
        w_hi, w_lo = split(jnp.where(grp < OV, vec[y, c, 0], 0.0))
        u_hi, u_lo = split(ur[y, c])
        return acc + nt(jnp.concatenate([w_hi, w_lo], 0), jnp.concatenate([u_hi, u_lo], 0))

    off = lax.fori_loop(0, per, off_body, jnp.zeros((2 * nk, 2 * nk), F32))
    off = off[:nk, :nk] + off[nk:, :nk] + off[:nk, nk:]
    gf[me, 0] = both
    gf[me, 1] = jnp.concatenate([off, jnp.zeros_like(off)], 1)
    grams = gather(gf, (gs_sem.at[STEPS], gr_sem.at[STEPS]), None)

    eye = (lax.broadcasted_iota(jnp.int32, (nk, 2 * nk), 0) + nk
           == lax.broadcasted_iota(jnp.int32, (nk, 2 * nk), 1)).astype(F32)
    right_half = lax.broadcasted_iota(jnp.int32, (nk, 2 * nk), 1) >= nk
    m = jnp.where(right_half, eye, grams[0])
    for j in range(nk):
        piv = m[j : j + 1, j : j + 1]
        line = m[j : j + 1, :]
        inv = 1.0 / piv
        m = jnp.where(
            ri > j, m - m[:, j : j + 1] * (line * inv), jnp.where(ri == j, line * lax.rsqrt(piv), m)
        )
    factor = m[:, nk:]
    fs[...] = m
    fcopy = to_next(fs, fr, us_sem.at[1], ur_sem.at[1])
    fcopy.start()
    diag_out[...] = exact(
        exact(factor, grams[0][:, nk:], ((1,), (0,))), factor, ((1,), (1,))
    )
    half_off = exact(factor, grams[1][:, :nk], ((1,), (0,)))

    for y_cp in back:
        y_cp.wait()
    f_hi, f_lo = split(factor)
    f3 = jnp.concatenate([f_hi, f_lo, f_hi], 1)
    home[me] = vec[me]

    def finish(i, _):
        c = lax.div(i, nq)
        q = i - c * nq
        w = jnp.concatenate([home[e, c, q] for e in range(n)], 1)
        w_hi, w_lo = split(w)
        z = jnp.dot(f3, jnp.concatenate([w_hi, w_hi, w_lo], 0), preferred_element_type=F32)
        blocks = [pltpu.roll(z[:, e * nz : (e + 1) * nz], e * group, 1) for e in range(n)]
        for r in range(n):
            res = blocks[0]
            for e in range(1, n):
                res = jnp.where(grp == (r + e) % n, blocks[e], res)
            res = pltpu.roll(res, ((n - r) % n) * group, 1)
            rows32[c, pl.ds(q * n + r, nk, stride=nx), :] = res
        return 0

    lax.fori_loop(0, comps * nq, finish, 0)
    for c in range(comps):
        out[c] = rows32[c].astype(BF16)
    fcopy.wait()
    off_res = exact(half_off, fr[:, nk:], ((1,), (1,)))
    off_out[...] = jnp.where(sub == 0, 0.0, off_res)


def on_device(n, subs, start, face_x, face_y, face_z, masses, active):
    _, comps, nk, rows, nx, nz = start.shape
    assert rows == 1 and nx % n == 0 and nz % n == 0 and n >= OV and n & (n - 1) == 0
    nq, group = nx // n, nz // n
    slots = -(-comps * nx // group)
    vm, dma = pltpu.VMEM, pltpu.SemaphoreType.DMA
    ph = STEPS + 1
    vmem = pl.BlockSpec(memory_space=pltpu.VMEM)
    big = (n, comps, nq, nk, nz)
    flat = lambda v: v.reshape(nx, nz)
    out, diag, off = pl.pallas_call(
        functools.partial(kernel, n, subs, comps, nk, nx),
        out_shape=(
            jax.ShapeDtypeStruct((comps, nk * nx, nz), BF16),
            jax.ShapeDtypeStruct((nk, nk), F32),
            jax.ShapeDtypeStruct((nk, nk), F32),
        ),
        in_specs=[vmem] * 5 + [pl.BlockSpec(memory_space=pltpu.SMEM)],
        out_specs=(vmem,) * 3,
        scratch_shapes=[
            vm(big, F32), vm(big, F32), vm(big, F32), vm(big, F32),
            vm((comps, nk * nx, nz), F32),
            vm((n, 6, nq, 8, nz), F32), vm((n, 6, nq, 8, nz), F32),
            vm((7, n, nq, 8, nz), F32),
            vm((ph, 2, slots, nk, nz), F32), vm((ph, 2, slots, nk, nz), F32),
            vm((STEPS, n, nk, 2 * nk), F32), vm((n, 2, nk, 2 * nk), F32),
            vm((n, comps, nk, nz), F32), vm((n, comps, nk, nz), F32),
            vm((nk, 2 * nk), F32), vm((nk, 2 * nk), F32),
            dma((comps, n)), dma((comps, n)), dma((n,)), dma((n,)),
            dma((ph, 2)), dma((ph, 2)), dma((ph, n)), dma((ph, n)),
            dma((n,)), dma((n,)), dma((2,)), dma((2,)),
        ],
        compiler_params=pltpu.CompilerParams(
            collective_id=0, has_side_effects=True, vmem_limit_bytes=48 * 2**20
        ),
    )(
        start.reshape(comps, nk * nx, nz),
        flat(face_x), flat(face_y), flat(face_z), flat(masses), active,
    )
    return out.reshape(start.shape), diag[None], off[None]


def solution(mesh):
    grid = P("sub", "dom", None, None)
    block = P("sub", None, None, "dom", None, None)
    return jax.shard_map(
        functools.partial(on_device, mesh.shape["dom"], mesh.shape["sub"]),
        mesh=mesh,
        in_specs=(block, grid, grid, grid, grid, P("sub")),
        out_specs=(block, P("sub", None, None), P("sub", None, None)),
        check_vma=False,
    )
```

time: 334 us -> 114 us (0.34)
  waiting for transfers between devices: 151 us -> 0 us
  Pallas kernels: 0 us -> 105 us
  blocking collectives: 75.8 us -> 0 us
  other arithmetic: 49.6 us -> 0 us
  starting transfers between devices: 25 us -> 0 us
  matrix products: 24.7 us -> 0 us
    ppermute x9 -> x0, waiting for transfers between devices: 151 us -> none  [the longest x3 103 us: with_halo(): lax.ppermute(head, axis, [((i + 1) % count, i) for i in range(ends)])]
    pallas_call x0 -> x1, Pallas kernels: none -> 105 us  [on_device(): pl.pallas_call(functools.partial(kernel, n, subs, comps, nk, nx), out_sha...]
    psum x3 -> x0, blocking collectives: 75.8 us -> none  [the longest x2 60 us: on_device(): lax.psum((gram_of(vectors, b_weight * vectors), gram_of(vectors, image_ra...]
    another operation x15 -> x0, other arithmetic: 36.2 us -> none  [the longest x9 19.6 us: inverse_factor(): factor = jnp.linalg.cholesky(gram_b)]
    ppermute x9 -> x0, starting transfers between devices: 25 us -> none  [the longest x3 12.7 us: with_halo(): lax.ppermute(tail, axis, [(i, (i + 1) % count) for i in range(ends)])]
    dot_general x22 -> x0, matrix products: 23.9 us -> none  [the longest x7 11.2 us: mix_cols(): jnp.einsum('ckyxz,kl->clyxz', values, matrix, precision=lax.Precision.HIG...]
    add x3 -> x0, other arithmetic: 7.21 us -> none  [operate(): result + face_terms(values, live_x, 3) + face_terms(values, live_z, 4)]
    mul x14 -> x0, other arithmetic: 6.01 us -> none  [the longest x3 3.67 us: on_device(): vectors = start * inside.astype(jnp.float32)[None, None]]
  transfers between devices with their start and end apart: 9 -> 0, of which waited for: 7 -> 0; matrix products, arithmetic and copies ran while one was open for 4% -> 0% of each run, Pallas kernels for 0% -> 0%
where the time goes in v1:
time: 114 us; the launch traced here: 113 us
  Pallas kernels  105 us (92%)
  local copies, waits for them, and re-layouts  6.3 us (6%)
  between operations  1.3 us (1%)
    pallas_call x1, Pallas kernels, on_device(): pl.pallas_call(functools.partial(kernel, n, subs, comps, nk, nx), out_sha...  105 us
    unnamed x13, local copies, waits for them, and re-layouts  6.3 us

profile of v1, /device:TPU:8, one launch (start us, length us, event | category | flops | bytes accessed | tf_op | source)
XLA Modules:
  0.0 112.6 jit_solution(6628075580665449424)
XLA Ops:
  1.3 0.0 copy-start
  1.3 1.4 %copy-done = f32[1,3,64,1,16,128]{5,4,3,2,1,0:T(8,128)S(1)} copy-done((f32[1,3,64,1,16,128]{5,4,3,2,1,0:T(8,128)S(1)}, f32[1,3,64,1,16,128]{5,4,3,2,1,0:T(8,128)}, u32[]{:S(2)}) %copy-start) | copy-done | bytes 1572888
  2.7 0.0 copy-start.1
  2.7 0.7 copy-done.1
  3.4 0.0 copy-start.2
  3.4 0.7 copy-done.2
  4.1 0.0 copy-start.3
  4.1 0.7 copy-done.3
  4.8 0.0 copy-start.4
  4.8 0.7 copy-done.4
  5.5 105.0 %shard_map.85 = (bf16[3,1024,128]{2,1,0:T(8,128)(2,1)S(1)}, f32[64,64]{1,0:T(8,128)S(1)}, f32[64,64]{1,0:T(8,128)S(1)}) custom-call(f32[3,1024,128]{2,1,0:T(8,128)S(1)} %bitcast.10, f32[16,128]{1,0:T(8,128)S(1)} %bitcast.14, f32[16,128]{1,0:T(8,128)S(1)} %bitcast.15, f32[16,128]{1,0:T(8,128)S(1)} %bitcast.16, f32[16,128]{1,0:T(8,128)S(1)} %bitcast.17, ...), custom_call_target="tpu_custom_call" | custom-call | tf_op jit(solution)/shard_map/pallas_call | solution.py:385
  110.5 0.9 copy.14
  111.4 0.6 copy.15
  112.0 0.6 copy.16
Async XLA Ops:
  1.3 1.4 %copy-start = (f32[1,3,64,1,16,128]{5,4,3,2,1,0:T(8,128)S(1)}, f32[1,3,64,1,16,128]{5,4,3,2,1,0:T(8,128)}, u32[]{:S(2)}) copy-start(f32[1,3,64,1,16,128]{5,4,3,2,1,0:T(8,128)} %param.6) | copy-start | bytes 4718596
  2.7 0.7 copy-start.1
  3.4 0.7 copy-start.2
  4.1 0.7 copy-start.3
  4.8 0.7 copy-start.4

commit v2 on v1

--- a/solution.py
+++ b/solution.py
@@ -31,16 +31,21 @@
 
 def kernel(
     n, subs, comps, nk, nx,
-    start, fx, fy, fz, mass, active,
+    start_hbm, fx, fy, fz, mass, active,
     out, diag_out, off_out,
-    sbuf, vec, img, home, rows32, cs, cr, dv, hs, hr, gr, gf, us, ur, fs, fr,
+    start, sbuf, vec, img, home, rows32, cs, cr, dv, hs, hr, gr, gf, us, ur, fs, fr,
     s_sem, r_sem, cs_sem, cr_sem, hs_sem, hr_sem, gs_sem, gr_sem,
-    ws_sem, wr_sem, us_sem, ur_sem,
+    ws_sem, wr_sem, us_sem, ur_sem, in_sem,
 ):
     nz = fx.shape[1]
     group = nz // n
     nq = nx // n
     per = n * comps
+    loads = [
+        pltpu.make_async_copy(start_hbm.at[c], start.at[c], in_sem.at[c]) for c in range(comps)
+    ]
+    for cp in loads:
+        cp.start()
     me = lax.axis_index("dom")
     sub = lax.axis_index("sub")
     peers = [lax.rem(me + d, n) for d in range(n)]
@@ -108,6 +113,8 @@
 
     vec_copies = []
     for c in range(comps):
+        loads[c].wait()
+
         def pack(q, _, c=c):
             blocks = []
             for r in range(n):
@@ -214,12 +221,16 @@
         acc = lax.fori_loop(0, per, body, jnp.zeros((2 * nk, 4 * nk), F32))
         return acc[:nk, : 2 * nk] + acc[:nk, 2 * nk :] + acc[nk:, : 2 * nk]
 
-    def gather(ref, sems, make):
+    def spread(ref, phase):
         copies = [
-            to_peer(ref.at[me], ref.at[me], sems[0].at[d], sems[1].at[d], d) for d in range(1, n)
+            to_peer(ref.at[me], ref.at[me], gs_sem.at[phase, d], gr_sem.at[phase, d], d)
+            for d in range(1, n)
         ]
         for cp in copies:
             cp.start()
+        return copies
+
+    def collect(ref, copies):
         for cp in copies:
             cp.wait()
         total = ref[0]
@@ -229,6 +240,10 @@
 
     hs[...] = jnp.zeros_like(hs)
     ri = lax.broadcasted_iota(jnp.int32, (nk, 1), 0)
+
+    def pair(m, j):
+        top, low = m[j : j + 1, :], m[j + 1 : j + 2, :]
+        return top, low, top[:, j : j + 1], top[:, j + 1 : j + 2], low[:, j + 1 : j + 2]
 
     def pack_halo(i, _):
         y = lax.div(i, comps)
@@ -246,11 +261,14 @@
         for cp in copies:
             cp.wait()
         gr[p, me] = apply_and_gram(p)
-        m = gather(gr.at[p], (gs_sem.at[p], gr_sem.at[p]), None)
-        for j in range(nk):
-            piv = m[j : j + 1, j : j + 1]
-            line = m[j : j + 1, :] / piv
-            m = jnp.where(ri == j, line, m - m[:, j : j + 1] * line)
+        m = collect(gr.at[p], spread(gr.at[p], p))
+        for j in range(0, nk, 2):
+            top, low, p00, p01, p11 = pair(m, j)
+            inv = 1.0 / (p00 * p11 - p01 * p01)
+            new_top = (p11 * inv) * top - (p01 * inv) * low
+            new_low = (p00 * inv) * low - (p01 * inv) * top
+            rest = m - m[:, j : j + 1] * new_top - m[:, j + 1 : j + 2] * new_low
+            m = jnp.where(ri == j, new_top, jnp.where(ri == j + 1, new_low, rest))
         xt = m.T[nk:, :]
         x_hi, x_lo = split(xt)
         x3 = jnp.concatenate([x_hi, x_lo, x_hi], 1)
@@ -287,7 +305,8 @@
         back.append(cp)
     for cp in copies:
         cp.wait()
-    both = apply_and_gram(STEPS)
+    gr[STEPS, me] = apply_and_gram(STEPS)
+    last_copies = spread(gr.at[STEPS], STEPS)
 
     r0 = lax.rem(a - OV, n)
 
@@ -308,6 +327,33 @@
     lax.fori_loop(0, per, planes, 0)
     ucopy = to_next(us, ur, us_sem.at[0], ur_sem.at[0])
     ucopy.start()
+    both = collect(gr.at[STEPS], last_copies)
+
+    eye = (lax.broadcasted_iota(jnp.int32, (nk, 2 * nk), 0) + nk
+           == lax.broadcasted_iota(jnp.int32, (nk, 2 * nk), 1)).astype(F32)
+    right_half = lax.broadcasted_iota(jnp.int32, (nk, 2 * nk), 1) >= nk
+    m = jnp.where(right_half, eye, both)
+    for j in range(0, nk, 2):
+        top, low, p00, p01, p11 = pair(m, j)
+        ratio = p01 / p00
+        second = low - ratio * top
+        p_second = p11 - ratio * p01
+        new_low = second / p_second
+        new_top = top / p00 - ratio * new_low
+        rest = m - m[:, j : j + 1] * new_top - m[:, j + 1 : j + 2] * new_low
+        m = jnp.where(
+            ri > j + 1,
+            rest,
+            jnp.where(
+                ri == j,
+                top * lax.rsqrt(p00),
+                jnp.where(ri == j + 1, second * lax.rsqrt(p_second), m),
+            ),
+        )
+    factor = m[:, nk:]
+    fs[...] = m
+    fcopy = to_next(fs, fr, us_sem.at[1], ur_sem.at[1])
+    fcopy.start()
     ucopy.wait()
 
     def off_body(i, acc):
@@ -319,29 +365,11 @@
 
     off = lax.fori_loop(0, per, off_body, jnp.zeros((2 * nk, 2 * nk), F32))
     off = off[:nk, :nk] + off[nk:, :nk] + off[:nk, nk:]
-    gf[me, 0] = both
-    gf[me, 1] = jnp.concatenate([off, jnp.zeros_like(off)], 1)
-    grams = gather(gf, (gs_sem.at[STEPS], gr_sem.at[STEPS]), None)
-
-    eye = (lax.broadcasted_iota(jnp.int32, (nk, 2 * nk), 0) + nk
-           == lax.broadcasted_iota(jnp.int32, (nk, 2 * nk), 1)).astype(F32)
-    right_half = lax.broadcasted_iota(jnp.int32, (nk, 2 * nk), 1) >= nk
-    m = jnp.where(right_half, eye, grams[0])
-    for j in range(nk):
-        piv = m[j : j + 1, j : j + 1]
-        line = m[j : j + 1, :]
-        inv = 1.0 / piv
-        m = jnp.where(
-            ri > j, m - m[:, j : j + 1] * (line * inv), jnp.where(ri == j, line * lax.rsqrt(piv), m)
-        )
-    factor = m[:, nk:]
-    fs[...] = m
-    fcopy = to_next(fs, fr, us_sem.at[1], ur_sem.at[1])
-    fcopy.start()
+    gf[me] = jnp.concatenate([off, jnp.zeros_like(off)], 1)
+    off_copies = spread(gf, STEPS + 1)
     diag_out[...] = exact(
-        exact(factor, grams[0][:, nk:], ((1,), (0,))), factor, ((1,), (1,))
+        exact(factor, both[:, nk:], ((1,), (0,))), factor, ((1,), (1,))
     )
-    half_off = exact(factor, grams[1][:, :nk], ((1,), (0,)))
 
     for y_cp in back:
         y_cp.wait()
@@ -368,6 +396,7 @@
     for c in range(comps):
         out[c] = rows32[c].astype(BF16)
     fcopy.wait()
+    half_off = exact(factor, collect(gf, off_copies)[:, :nk], ((1,), (0,)))
     off_res = exact(half_off, fr[:, nk:], ((1,), (1,)))
     off_out[...] = jnp.where(sub == 0, 0.0, off_res)
 
@@ -389,20 +418,21 @@
             jax.ShapeDtypeStruct((nk, nk), F32),
             jax.ShapeDtypeStruct((nk, nk), F32),
         ),
-        in_specs=[vmem] * 5 + [pl.BlockSpec(memory_space=pltpu.SMEM)],
+        in_specs=[pl.BlockSpec(memory_space=pltpu.HBM)] + [vmem] * 4 + [pl.BlockSpec(memory_space=pltpu.SMEM)],
         out_specs=(vmem,) * 3,
         scratch_shapes=[
+            vm((comps, nk * nx, nz), F32),
             vm(big, F32), vm(big, F32), vm(big, F32), vm(big, F32),
             vm((comps, nk * nx, nz), F32),
             vm((n, 6, nq, 8, nz), F32), vm((n, 6, nq, 8, nz), F32),
             vm((7, n, nq, 8, nz), F32),
             vm((ph, 2, slots, nk, nz), F32), vm((ph, 2, slots, nk, nz), F32),
-            vm((STEPS, n, nk, 2 * nk), F32), vm((n, 2, nk, 2 * nk), F32),
+            vm((ph, n, nk, 2 * nk), F32), vm((n, nk, 2 * nk), F32),
             vm((n, comps, nk, nz), F32), vm((n, comps, nk, nz), F32),
             vm((nk, 2 * nk), F32), vm((nk, 2 * nk), F32),
             dma((comps, n)), dma((comps, n)), dma((n,)), dma((n,)),
-            dma((ph, 2)), dma((ph, 2)), dma((ph, n)), dma((ph, n)),
-            dma((n,)), dma((n,)), dma((2,)), dma((2,)),
+            dma((ph, 2)), dma((ph, 2)), dma((ph + 1, n)), dma((ph + 1, n)),
+            dma((n,)), dma((n,)), dma((2,)), dma((2,)), dma((comps,)),
         ],
         compiler_params=pltpu.CompilerParams(
             collective_id=0, has_side_effects=True, vmem_limit_bytes=48 * 2**20

time: 114 us -> 118 us (1.035)
  Pallas kernels: 105 us -> 110 us
    pallas_call x1, Pallas kernels: 105 us -> 110 us  [on_device(): pl.pallas_call(functools.partial(kernel, n, subs, comps, nk, nx), out_sha...]
where the time goes in v2:
time: 118 us; the launch traced here: 117 us
  Pallas kernels  110 us (93%)
  local copies, waits for them, and re-layouts  6.3 us (5%)
  between operations  1.3 us (1%)
    pallas_call x1, Pallas kernels, on_device(): pl.pallas_call(functools.partial(kernel, n, subs, comps, nk, nx), out_sha...  110 us
    unnamed x13, local copies, waits for them, and re-layouts  6.3 us

profile of v2, /device:TPU:8, one launch (start us, length us, event | category | flops | bytes accessed | tf_op | source)
XLA Modules:
  0.0 117.3 jit_solution(14713739931594431759)
XLA Ops:
  1.3 0.0 copy-start
  1.3 1.4 %copy-done = f32[1,3,64,1,16,128]{5,4,3,2,1,0:T(8,128)S(1)} copy-done((f32[1,3,64,1,16,128]{5,4,3,2,1,0:T(8,128)S(1)}, f32[1,3,64,1,16,128]{5,4,3,2,1,0:T(8,128)}, u32[]{:S(2)}) %copy-start) | copy-done | bytes 1572888
  2.7 0.0 copy-start.1
  2.7 0.7 copy-done.1
  3.4 0.0 copy-start.2
  3.4 0.7 copy-done.2
  4.1 0.0 copy-start.3
  4.1 0.7 copy-done.3
  4.8 0.0 copy-start.4
  4.8 0.7 copy-done.4
  5.5 109.7 %shard_map.85 = (bf16[3,1024,128]{2,1,0:T(8,128)(2,1)S(1)}, f32[64,64]{1,0:T(8,128)S(1)}, f32[64,64]{1,0:T(8,128)S(1)}) custom-call(f32[3,1024,128]{2,1,0:T(8,128)S(1)} %bitcast.10, f32[16,128]{1,0:T(8,128)S(1)} %bitcast.14, f32[16,128]{1,0:T(8,128)S(1)} %bitcast.15, f32[16,128]{1,0:T(8,128)S(1)} %bitcast.16, f32[16,128]{1,0:T(8,128)S(1)} %bitcast.17, ...), custom_call_target="tpu_custom_call" | custom-call | tf_op jit(solution)/shard_map/pallas_call | solution.py:414
  115.2 0.9 copy.14
  116.1 0.6 copy.15
  116.7 0.6 copy.16
Async XLA Ops:
  1.3 1.4 %copy-start = (f32[1,3,64,1,16,128]{5,4,3,2,1,0:T(8,128)S(1)}, f32[1,3,64,1,16,128]{5,4,3,2,1,0:T(8,128)}, u32[]{:S(2)}) copy-start(f32[1,3,64,1,16,128]{5,4,3,2,1,0:T(8,128)} %param.6) | copy-start | bytes 4718596
  2.7 0.7 copy-start.1
  3.4 0.7 copy-start.2
  4.1 0.7 copy-start.3
  4.8 0.7 copy-start.4

commit v3 on v2

--- a/solution.py
+++ b/solution.py
@@ -241,10 +241,6 @@
     hs[...] = jnp.zeros_like(hs)
     ri = lax.broadcasted_iota(jnp.int32, (nk, 1), 0)
 
-    def pair(m, j):
-        top, low = m[j : j + 1, :], m[j + 1 : j + 2, :]
-        return top, low, top[:, j : j + 1], top[:, j + 1 : j + 2], low[:, j + 1 : j + 2]
-
     def pack_halo(i, _):
         y = lax.div(i, comps)
         c = i - y * comps
@@ -262,13 +258,10 @@
             cp.wait()
         gr[p, me] = apply_and_gram(p)
         m = collect(gr.at[p], spread(gr.at[p], p))
-        for j in range(0, nk, 2):
-            top, low, p00, p01, p11 = pair(m, j)
-            inv = 1.0 / (p00 * p11 - p01 * p01)
-            new_top = (p11 * inv) * top - (p01 * inv) * low
-            new_low = (p00 * inv) * low - (p01 * inv) * top
-            rest = m - m[:, j : j + 1] * new_top - m[:, j + 1 : j + 2] * new_low
-            m = jnp.where(ri == j, new_top, jnp.where(ri == j + 1, new_low, rest))
+        for j in range(nk):
+            piv = m[j : j + 1, j : j + 1]
+            line = m[j : j + 1, :] / piv
+            m = jnp.where(ri == j, line, m - m[:, j : j + 1] * line)
         xt = m.T[nk:, :]
         x_hi, x_lo = split(xt)
         x3 = jnp.concatenate([x_hi, x_lo, x_hi], 1)
@@ -333,22 +326,12 @@
            == lax.broadcasted_iota(jnp.int32, (nk, 2 * nk), 1)).astype(F32)
     right_half = lax.broadcasted_iota(jnp.int32, (nk, 2 * nk), 1) >= nk
     m = jnp.where(right_half, eye, both)
-    for j in range(0, nk, 2):
-        top, low, p00, p01, p11 = pair(m, j)
-        ratio = p01 / p00
-        second = low - ratio * top
-        p_second = p11 - ratio * p01
-        new_low = second / p_second
-        new_top = top / p00 - ratio * new_low
-        rest = m - m[:, j : j + 1] * new_top - m[:, j + 1 : j + 2] * new_low
+    for j in range(nk):
+        piv = m[j : j + 1, j : j + 1]
+        line = m[j : j + 1, :]
+        inv = 1.0 / piv
         m = jnp.where(
-            ri > j + 1,
-            rest,
-            jnp.where(
-                ri == j,
-                top * lax.rsqrt(p00),
-                jnp.where(ri == j + 1, second * lax.rsqrt(p_second), m),
-            ),
+            ri > j, m - m[:, j : j + 1] * (line * inv), jnp.where(ri == j, line * lax.rsqrt(piv), m)
         )
     factor = m[:, nk:]
     fs[...] = m

time: 118 us -> 114 us (0.966)
  Pallas kernels: 110 us -> 106 us
    pallas_call x1, Pallas kernels: 110 us -> 106 us  [on_device(): pl.pallas_call(functools.partial(kernel, n, subs, comps, nk, nx), out_sha...]
where the time goes in v3:
time: 114 us; the launch traced here: 113 us
  Pallas kernels  106 us (93%)
  local copies, waits for them, and re-layouts  6.3 us (6%)
  between operations  1.3 us (1%)
    pallas_call x1, Pallas kernels, on_device(): pl.pallas_call(functools.partial(kernel, n, subs, comps, nk, nx), out_sha...  106 us
    unnamed x13, local copies, waits for them, and re-layouts  6.3 us

profile of v3, /device:TPU:8, one launch (start us, length us, event | category | flops | bytes accessed | tf_op | source)
XLA Modules:
  0.0 113.4 jit_solution(12758138718743459212)
XLA Ops:
  1.3 0.0 copy-start
  1.3 1.4 %copy-done = f32[1,3,64,1,16,128]{5,4,3,2,1,0:T(8,128)S(1)} copy-done((f32[1,3,64,1,16,128]{5,4,3,2,1,0:T(8,128)S(1)}, f32[1,3,64,1,16,128]{5,4,3,2,1,0:T(8,128)}, u32[]{:S(2)}) %copy-start) | copy-done | bytes 1572888
  2.7 0.0 copy-start.1
  2.7 0.7 copy-done.1
  3.4 0.0 copy-start.2
  3.4 0.7 copy-done.2
  4.1 0.0 copy-start.3
  4.1 0.7 copy-done.3
  4.8 0.0 copy-start.4
  4.8 0.7 copy-done.4
  5.5 105.8 %shard_map.85 = (bf16[3,1024,128]{2,1,0:T(8,128)(2,1)S(1)}, f32[64,64]{1,0:T(8,128)S(1)}, f32[64,64]{1,0:T(8,128)S(1)}) custom-call(f32[3,1024,128]{2,1,0:T(8,128)S(1)} %bitcast.10, f32[16,128]{1,0:T(8,128)S(1)} %bitcast.14, f32[16,128]{1,0:T(8,128)S(1)} %bitcast.15, f32[16,128]{1,0:T(8,128)S(1)} %bitcast.16, f32[16,128]{1,0:T(8,128)S(1)} %bitcast.17, ...), custom_call_target="tpu_custom_call" | custom-call | tf_op jit(solution)/shard_map/pallas_call | solution.py:397
  111.3 0.9 copy.14
  112.2 0.6 copy.15
  112.8 0.6 copy.16
Async XLA Ops:
  1.3 1.4 %copy-start = (f32[1,3,64,1,16,128]{5,4,3,2,1,0:T(8,128)S(1)}, f32[1,3,64,1,16,128]{5,4,3,2,1,0:T(8,128)}, u32[]{:S(2)}) copy-start(f32[1,3,64,1,16,128]{5,4,3,2,1,0:T(8,128)} %param.6) | copy-start | bytes 4718596
  2.7 0.7 copy-start.1
  3.4 0.7 copy-start.2
  4.1 0.7 copy-start.3
  4.8 0.7 copy-start.4
